TPU v7x, 32 devices: a whole 2x2x4 slice. The times are simulated.
32 devices in a mesh: groups: 2 (over x), ctx: 16 (over z, y, core).
Axes of the slice: x: 2, y: 2, z: 4, core: 2. Of those that a mesh axis runs over, the one named last changes fastest.
Arguments:
- values: bfloat16 [4096, 4096], P(('groups', 'ctx')), parts along dimension 0, may hold values from -6 to 6
- in_b: bfloat16 [4096, 512], P(('groups', 'ctx')), parts along dimension 0, may hold values from -0.75 to 0.75
- out_c: bfloat16 [4096, 512], P(('groups', 'ctx')), parts along dimension 0, may hold values from -6 to 6
- decay_log: float32 [64, 4096], P(None, ('groups', 'ctx')), parts along dimension 1, may hold values from -1 to 0
- residual: bfloat16 [4096, 4096], P(('groups', 'ctx')), parts along dimension 0, may hold values from -40 to 40
- mixer_gain: float32 [4096], replicated, may hold values from 0.5 to 1.5
- moe_gain: float32 [4096], replicated, may hold values from 0.5 to 1.5
- w_down: bfloat16 [4096, 1024], P('ctx'), may hold values from -0.09375 to 0.09375
- w_in: bfloat16 [16, 1024, 1024], P('ctx'), may hold values from -0.1875 to 0.1875
- w_out: bfloat16 [16, 1024, 1024], P('ctx'), may hold values from -0.1875 to 0.1875
- routes: int32 [4096, 6], P(('groups', 'ctx')), parts along dimension 0, may hold values from 0 to 15, all different within a row; in each aligned block of 128 rows (0 to 127, 128 to 255, ...) at most 72 rows name the same one
- gate_int: int32 [4096, 6], P(('groups', 'ctx')), parts along dimension 0, may hold values from 1 to 16
Outputs:
- mixed: bfloat16 [4096, 4096], P(('groups', 'ctx')), parts along dimension 0
- latent_mix: bfloat16 [4096, 1024], P(('groups', 'ctx')), parts along dimension 0
There are 2 independent parts, one for each index of `groups`. A program takes and returns all parts, laid end to end along the dimension named above; an argument that names none is the same for every part. Nothing has to cross between parts.
Inputs may be any that keep to these rules, and one draw needn't show every extreme that they name: `routes`: each row names 6 different experts; within the 128 rows of one device, no expert is named more than 72 times, a bound that some block reaches.
All inputs are finite; a program needn't handle non-finite values.
Results may differ from a plain program's by a relative error of at most 0.013.
Values may be sent and summed in bfloat16 or wider, within the bound.
A program may use at most 320 MiB of HBM per device.

v0:
```python
import jax
import jax.numpy as jnp
from jax import lax
from jax.sharding import PartitionSpec as P

D = 4096
MIXER_HEADS = 64
P_SIZE = 64
N = 64
GROUPS = 8
L = 1024


def prefix(array, axis, combine, identity):
    count, index = (lax.axis_size(axis), lax.axis_index(axis))
    everything = jax.tree.map(lambda part: lax.all_gather(part, axis), array)
    start = jax.tree.map(
        lambda part, zero: jnp.broadcast_to(jnp.asarray(zero, part.dtype), part.shape),
        array,
        identity,
    )

    def step(k, before):
        reached = k < index
        new = combine(before, jax.tree.map(lambda part: part[k], everything))
        return jax.tree.map(lambda a, b: jnp.where(reached, a, b), new, before)

    return lax.fori_loop(0, count, step, start)


def block_terms(block_values, block_in, block_out, block_logs):
    running = jnp.cumsum(block_logs, axis=-1)
    scores = jnp.einsum("tgn,sgn->gts", block_out, block_in, preferred_element_type=jnp.float32)
    length = block_logs.shape[-1]
    lower = jnp.arange(length)[:, None] >= jnp.arange(length)[None, :]
    spread = running[..., :, None] - running[..., None, :]
    decays = jnp.where(lower, jnp.exp(jnp.where(lower, spread, 0.0)), 0.0)
    weights = (scores[:, None] * decays).astype(jnp.bfloat16)
    inner = jnp.einsum("ghts,sghp->tghp", weights, block_values, preferred_element_type=jnp.float32)
    tails = jnp.exp(running[..., -1:] - running)
    scaled = (block_values.astype(jnp.float32) * jnp.transpose(tails, (2, 0, 1))[..., None]).astype(
        jnp.bfloat16
    )
    update = jnp.einsum("sghp,sgn->ghpn", scaled, block_in, preferred_element_type=jnp.float32)
    return (running, inner, update)


def carry_term(running, block_out, carried):
    reach = jnp.einsum(
        "tgn,ghpn->tghp", block_out.astype(jnp.float32), carried, precision=lax.Precision.HIGHEST
    )
    return jnp.transpose(jnp.exp(running), (2, 0, 1))[..., None] * reach


def chain_combine(earlier, later):
    return (earlier[0] + later[0], jnp.exp(later[0])[..., None, None] * earlier[1] + later[1])


def on_device(
    values,
    in_b,
    out_c,
    decay_log,
    residual,
    mixer_gain,
    moe_gain,
    w_down,
    w_in,
    w_out,
    routes,
    gate_int,
):
    tok_count = values.shape[0]
    devices = lax.axis_size("ctx")
    per_group = MIXER_HEADS // GROUPS
    value_rows = values.reshape(tok_count, GROUPS, per_group, P_SIZE)
    in_rows = in_b.reshape(tok_count, GROUPS, N)
    out_rows = out_c.reshape(tok_count, GROUPS, N)
    log_rows = decay_log.reshape(GROUPS, per_group, tok_count)
    carried = jnp.zeros((GROUPS, per_group, P_SIZE, N), jnp.float32)
    total_log = jnp.zeros((GROUPS, per_group), jnp.float32)
    offset = 0
    running, inner, update = block_terms(value_rows, in_rows, out_rows, log_rows)
    saved_blocks = (offset, running, inner, carried, total_log)
    carried = jnp.exp(running[..., -1])[..., None, None] * carried + update
    total_log = running[..., -1]
    identity = (jnp.zeros_like(total_log), jnp.zeros_like(carried))
    incoming = prefix((total_log, carried), "ctx", chain_combine, identity)[1]
    offset, running, inner, before, before_log = saved_blocks
    entering = before + jnp.exp(before_log)[..., None, None] * incoming
    outputs = inner + carry_term(running, out_rows, entering)
    heads_out = outputs.reshape(tok_count, MIXER_HEADS, P_SIZE)
    scale = lax.rsqrt(jnp.mean(heads_out * heads_out, axis=-1, keepdims=True) + 1e-05)
    normed_heads = (heads_out * scale * mixer_gain.reshape(MIXER_HEADS, P_SIZE)).reshape(
        tok_count, D
    )
    mixed = (residual.astype(jnp.float32) + normed_heads).astype(jnp.bfloat16)
    wide = mixed.astype(jnp.float32)
    normed = (
        wide * lax.rsqrt(jnp.mean(wide * wide, axis=-1, keepdims=True) + 1e-05) * moe_gain
    ).astype(jnp.bfloat16)
    whole_down = lax.all_gather(w_down, "ctx", axis=0, tiled=True)
    latent = jnp.dot(normed, whole_down, preferred_element_type=jnp.float32).astype(jnp.bfloat16)
    local_count = w_in.shape[0]
    experts = local_count * devices
    choices = routes.shape[1]
    capacity = 8 * max(1, (3 * tok_count * choices // (2 * experts) + 7) // 8)
    flat_routes = routes.reshape(-1)
    onehot = (flat_routes[:, None] == jnp.arange(experts, dtype=jnp.int32)[None, :]).astype(
        jnp.int32
    )
    slot_index = jnp.sum((jnp.cumsum(onehot, axis=0) - onehot) * onehot, axis=1)
    targets = flat_routes * capacity + slot_index
    sent_rows = jnp.repeat(latent, choices, axis=0)
    outgoing = (
        jnp.zeros((experts * capacity, L), jnp.bfloat16)
        .at[targets]
        .set(sent_rows)
        .reshape(experts, capacity, L)
    )
    arrived = lax.all_to_all(outgoing, "ctx", split_axis=0, concat_axis=0, tiled=True)
    slot_count = arrived.shape[1]
    grouped = arrived.reshape(devices, local_count, slot_count, L)
    hidden_act = jnp.einsum("jecl,elf->jecf", grouped, w_in, preferred_element_type=jnp.float32)
    hidden_act = jnp.square(jax.nn.relu(hidden_act)).astype(jnp.bfloat16)
    produced = jnp.einsum(
        "jecf,efl->jecl", hidden_act, w_out, preferred_element_type=jnp.float32
    ).astype(jnp.bfloat16)
    returned = lax.all_to_all(
        produced.reshape(devices * local_count, slot_count, L),
        "ctx",
        split_axis=0,
        concat_axis=0,
        tiled=True,
    )
    picked = returned.reshape(experts * capacity, L)[targets].reshape(tok_count, choices, L)
    gate_float = gate_int.astype(jnp.float32)
    gate = gate_float / jnp.sum(gate_float, axis=1, keepdims=True)
    latent_mix = jnp.sum(picked.astype(jnp.float32) * gate[..., None], axis=1).astype(jnp.bfloat16)
    return (mixed, latent_mix)


def solution(mesh):
    return jax.shard_map(
        on_device,
        mesh=mesh,
        in_specs=(
            P(("groups", "ctx"), None),
            P(("groups", "ctx"), None),
            P(("groups", "ctx"), None),
            P(None, ("groups", "ctx")),
            P(("groups", "ctx"), None),
            P(),
            P(),
            P("ctx", None),
            P("ctx", None, None),
            P("ctx", None, None),
            P(("groups", "ctx"), None),
            P(("groups", "ctx"), None),
        ),
        out_specs=(P(("groups", "ctx"), None), P(("groups", "ctx"), None)),
        check_vma=False,
    )
```

profile of v0, /device:TPU:0, one launch (start us, length us, event | category | flops | bytes accessed | tf_op | source)
XLA Modules:
  0.0 422.7 jit_solution(7598415168407967290)
XLA Ops:
  7.2 4.3 %reduce_window_sum.26 = f32[8,8,128]{2,1,0:T(8,128)S(1)} reduce-window(f32[8,8,128]{2,1,0:T(8,128)} %bitcast.101, f32[]{:T(128)} %constant.47.clone.1), window={size=1x1x128 pad=0_0x0_0x127_0}, to_apply=%region_0.0 | reduce-window | flops 1040384 | bytes 65540 | tf_op jit(solution)/shard_map/jit(cumsum)/reduce_window_sum | solution.py:32
  12.3 1.6 copy.35
  14.1 1.8 convolution_add_fusion
  15.9 0.7 all-gather.5.cloned.1.call-update
  16.9 0.7 eq.25
  17.6 0.7 copy.36
  18.3 1.0 copy.33
  19.4 2.3 copy.32
  21.6 1.7 reduce-window.6
  24.8 0.8 copy.39
  25.6 0.7 mul.141
  26.3 23.9 %all-gather = f32[128,8,1]{1,2,0:T(1,128)S(1)} all-gather(f32[8,8,1]{1,2,0:T(1,128)} %copy.36), channel_id=2, replica_groups=mesh['groups'=2,'ctx'=16] {'ctx'}, dimensions={0}, use_global_device_ids=true | all-gather | bytes 4352 | tf_op jit(solution)/shard_map/all_gather | solution.py:16
  50.3 0.8 fusion.34
  51.1 0.7 fusion.36
  52.1 3.3 fusion.3
  55.4 131.7 %all-gather.7.cloned.1.call-done = f32[128,8,64,64]{3,2,1,0:T(8,128)} async-done(((f32[8,8,64,64]{3,2,1,0:T(8,128)}), f32[128,8,64,64]{3,2,1,0:T(8,128)}) %all-gather.7.cloned.1.call-update) | async-done | bytes 16777232 | tf_op jit(solution)/shard_map/all_gather | solution.py:16
  187.1 61.2 %while.14 = (s32[]{:T(128)}, f32[8,8,64,64]{3,2,1,0:T(8,128)}, s32[]{:T(128)}, f32[16,8,8]{2,1,0:T(8,128)S(1)}, f32[16,8,8,64,64]{4,3,2,1,0:T(8,128)}, /*index=5*/s32[]{:T(128)}, s32[]{:T(128)}) while((s32[]{:T(128)}, f32[8,8,64,64]{3,2,1,0:T(8,128)}, s32[]{:T(128)}, f32[16,8,8]{2,1,0:T(8,128)S(1)}, ...), condition=%wide.region_2.3_spmd.clone, body=%wide.region_1.2_spmd.clone.sunk | while | flops 1048580 | bytes 3146601 | solution.py:28
  187.1 3.2 fusion.50
  190.3 3.8 fusion.50
  194.1 3.8 fusion.50
  198.0 4.0 fusion.50
  202.0 3.9 fusion.50
  205.8 3.9 fusion.50
  209.7 3.9 fusion.50
  213.6 3.9 fusion.50
  217.4 3.8 fusion.50
  221.3 3.9 fusion.50
  225.1 3.8 fusion.50
  229.0 3.9 fusion.50
  232.9 3.9 fusion.50
  236.7 3.9 fusion.50
  240.6 3.8 fusion.50
  244.5 3.8 fusion.50
  248.3 4.1 multiply_reduce_fusion.1
  252.5 0.9 fusion.4
  253.4 11.1 %all-gather.5.cloned.1.call-done = bf16[4096,1024]{1,0:T(8,128)(2,1)} async-done(((bf16[256,1024]{1,0:T(8,128)(2,1)}), bf16[4096,1024]{1,0:T(8,128)(2,1)}) %all-gather.5.cloned.1.call-update) | async-done | bytes 8388624 | tf_op jit(solution)/shard_map/all_gather | solution.py:102
  264.5 5.7 %convolution_convert_fusion = bf16[128,1024]{1,0:T(8,128)(2,1)S(1)} fusion(bf16[4096,1024]{1,0:T(8,128)(2,1)} %all-gather.5.cloned.1.call-done, bf16[128,4096]{0,1:T(8,128)(2,1)S(1)} %get-tuple-element.140, f32[4096]{0:T(1024)S(1)} %copy-done.5, f32[128]{0:T(128)S(1)} %add_rsqrt_fusion), kind=kOutput, calls=%fused_computation.34 | convolution fusion | flops 1075970048 | bytes 9716224 | tf_op jit(solution)/shard_map/dot_general | solution.py:103
  270.2 1.7 broadcast_in_dim.22
  271.9 3.7 reshape.171
  275.6 8.1 %scatter_custom_fusion = bf16[1152,1024]{1,0:T(8,128)(2,1)} fusion(s32[768]{0:T(1024)S(1)} %fusion.36, bf16[768,1024]{1,0:T(8,128)(2,1)} %reshape.171, bf16[]{:T(256)} %constant.52.clone.1), kind=kCustom, calls=%fused_computation.35 | custom fusion | bytes 2359808 | tf_op jit(solution)/shard_map/scatter | solution.py:118
  283.7 58.4 %all_to_all.10 = bf16[16,72,1024]{2,1,0:T(8,128)(2,1)} all-to-all(bf16[16,72,1024]{2,1,0:T(8,128)(2,1)} %bitcast.92), channel_id=1, replica_groups=mesh['groups'=2,'ctx'=16] {'ctx'}, dimensions={0} | all-to-all | bytes 4718592 | tf_op jit(solution)/shard_map/all_to_all | solution.py:121
  342.1 8.8 %fusion.19 = bf16[16,72,1024]{2,1,0:T(8,128)(2,1)} fusion(bf16[1,1024,1024]{2,1,0:T(8,128)(2,1)S(1)} %copy-done, bf16[16,72,1024]{2,1,0:T(8,128)(2,1)} %all_to_all.10, bf16[1,1024,1024]{2,1,0:T(8,128)(2,1)} %param.22), kind=kOutput, calls=%fused_computation.32 | convolution fusion | flops 4836556800 | bytes 8912896 | tf_op jit(solution)/shard_map/jecf,efl->jecl/dot_general | solution.py:126
  350.9 4.6 %all-to-all-start.1 = ((bf16[16,72,1024]{2,1,0:T(8,128)(2,1)}), bf16[16,72,1024]{2,1,0:T(8,128)(2,1)}, u32[]{:S(2)}, u32[]{:S(2)}) async-start(bf16[16,72,1024]{2,1,0:T(8,128)(2,1)} %fusion.19), calls=%async_computation.1 | async-start | bytes 4718592 | tf_op jit(solution)/shard_map/all_to_all | solution.py:129
  355.7 1.3 copy.44
  357.0 44.2 %all-to-all-done.1 = bf16[16,72,1024]{2,1,0:T(8,128)(2,1)} async-done(((bf16[16,72,1024]{2,1,0:T(8,128)(2,1)}), bf16[16,72,1024]{2,1,0:T(8,128)(2,1)}, u32[]{:S(2)}, u32[]{:S(2)}) %all-to-all-start.1) | async-done | bytes 2359328 | tf_op jit(solution)/shard_map/all_to_all | solution.py:129
  401.1 6.5 %gather_fusion = bf16[768,1024]{1,0:T(8,128)(2,1)} fusion(bf16[1152,1024]{1,0:T(8,128)(2,1)} %bitcast.23, s32[1024]{0:T(1024)S(1)} %pad_clamp_fusion), kind=kCustom, calls=%fused_computation | custom fusion | bytes 3148800 | tf_op jit(solution)/shard_map/gather | solution.py:136
  407.7 3.9 reshape.158
  411.6 4.3 %multiply_reduce_fusion = bf16[128,1024]{1,0:T(8,128)(2,1)} fusion(f32[128,6,1024]{2,1,0:T(8,128)} %reshape.158, f32[128,6]{1,0:T(8,128)S(1)} %copy.43), kind=kLoop, calls=%fused_computation.6 | loop fusion | flops 1441792 | bytes 3410944 | tf_op jit(solution)/shard_map/reduce_sum | solution.py:139
  (54 shorter events, 3.3 us)
Async XLA Ops:
  7.2 334.9 %copy-start = (bf16[1,1024,1024]{2,1,0:T(8,128)(2,1)S(1)}, bf16[1,1024,1024]{2,1,0:T(8,128)(2,1)}, u32[]{:S(2)}) copy-start(bf16[1,1024,1024]{2,1,0:T(8,128)(2,1)} %param.23) | copy-start | bytes 6291460
  7.2 6.8 %copy-start.3 = (bf16[128,512]{1,0:T(8,128)(2,1)S(1)}, bf16[128,512]{1,0:T(8,128)(2,1)}, u32[]{:S(2)}) copy-start(bf16[128,512]{1,0:T(8,128)(2,1)} %param.15) | copy-start | bytes 393220
  7.2 179.9 %all-gather.7.cloned.1.call-start = ((), (), s32[]{:S(2)}) async-start(), calls=%async_computation.3 | async-start | bytes 35651584 | tf_op jit(solution)/shard_map/all_gather | solution.py:16
  15.9 0.8 copy-start.6
  15.9 248.6 %all-gather.5.cloned.1.call-start = ((), (), s32[]{:S(2)}) async-start(), calls=%async_computation.2 | async-start | bytes 8912896 | tf_op jit(solution)/shard_map/all_gather | solution.py:102
  187.1 61.3 %copy-start.2 = (f32[128,8,8]{0,2,1:T(8,128)S(1)}, f32[128,8,8]{0,2,1:T(8,128)}, u32[]{:S(2)}) copy-start(f32[128,8,8]{0,2,1:T(8,128)} %get-tuple-element.141) | copy-start | bytes 98308
  248.3 4.1 copy-start.1
  248.3 4.1 copy-start.4
  252.5 12.1 %copy-start.5 = (f32[4096]{0:T(1024)S(1)}, f32[4096]{0:T(1024)}, u32[]{:S(2)}) copy-start(f32[4096]{0:T(1024)} %param.20) | copy-start | bytes 49156
  350.9 4.6 %copy-start.7 = (s32[128,6]{0,1:T(8,128)S(1)}, s32[128,6]{0,1:T(8,128)}, u32[]{:S(2)}) copy-start(s32[128,6]{0,1:T(8,128)} %param.25) | copy-start | bytes 9220
  350.9 50.2 %all-to-all-start.1 = ((bf16[16,72,1024]{2,1,0:T(8,128)(2,1)}), bf16[16,72,1024]{2,1,0:T(8,128)(2,1)}, u32[]{:S(2)}, u32[]{:S(2)}) async-start(bf16[16,72,1024]{2,1,0:T(8,128)(2,1)} %fusion.19), calls=%async_computation.1 | async-start | bytes 4718592 | tf_op jit(solution)/shard_map/all_to_all | solution.py:129
Sparse Core Ops, SparseCore 0:
  16.0 171.0 all-gather.6
  189.2 75.2 all-gather.4
where the time goes:
time: 430 us; the launch traced here: 423 us
  waiting for transfers between devices  188 us (44%)
  blocking collectives  82.3 us (19%)
  other arithmetic  75.8 us (18%)
  local copies, waits for them, and re-layouts  34 us (8%)
  matrix products  23.9 us (6%)
  between operations  14.2 us (3%)
  starting transfers between devices  4.65 us (1%)
    all_gather x1, waiting for transfers between devices, prefix(): everything = jax.tree.map(lambda part: lax.all_gather(part, axis), array)  132 us
    select_n x16, other arithmetic, step(): return jax.tree.map(lambda a, b: jnp.where(reached, a, b), new, before)  61.2 us
    all_to_all x1, blocking collectives, on_device(): lax.all_to_all(outgoing, 'ctx', split_axis=0, concat_axis=0, tiled=True)  58.4 us
    all_to_all x1, waiting for transfers between devices, on_device(): lax.all_to_all(produced.reshape(devices * local_count, slot_count, L), 'c...  44.2 us
    all_gather x1, blocking collectives, prefix(): everything = jax.tree.map(lambda part: lax.all_gather(part, axis), array)  23.9 us
    all_gather x1, waiting for transfers between devices, on_device(): whole_down = lax.all_gather(w_down, 'ctx', axis=0, tiled=True)  11.1 us
    dot_general x1, matrix products, on_device(): jnp.einsum('jecf,efl->jecl', hidden_act, w_out, preferred_element_type=jn...  8.82 us
  transfers between devices with their start and end apart: 3, of which 3 were waited for; matrix products, arithmetic and copies ran while one was open for 20% of the time, Pallas kernels for 0%

commit v1 on v0

v1 whole, which is shorter than its diff:
```python
import functools

import jax
import jax.numpy as jnp
from jax import lax
from jax.experimental import pallas as pl
from jax.experimental.pallas import tpu as pltpu
from jax.sharding import PartitionSpec as P

P_SIZE = 64
N = 64
GROUPS = 8
EXTRA = 16
MESH = pl.DeviceIdType.MESH
F32 = jnp.float32
BF16 = jnp.bfloat16


def ring_place(chips, chip):
    if chips == 8:
        z, y = chip // 2, chip % 2
        return z * (1 - y) + (7 - z) * y
    return chip


def ring_chip(chips, place):
    place = lax.rem(place + 2 * chips, chips)
    if chips == 8:
        back = place // 4
        return (1 - back) * (2 * place) + back * (2 * (7 - place) + 1)
    return place


def remote(src, dst, send, recv, device):
    return pltpu.make_async_remote_copy(
        src_ref=src,
        dst_ref=dst,
        send_sem=send,
        recv_sem=recv,
        device_id={"ctx": device},
        device_id_type=MESH,
    )


class Gather:
    def __init__(self, buf, chips, place, core, sems):
        self.buf, self.chips, self.place, self.core = buf, chips, place, core
        self.half = chips // 2
        self.rows = buf.shape[1]
        self.ring_send, self.ring_recv, self.side_send, self.side_recv = sems
        self.started = []

    def slot(self, place, core=None):
        return ring_chip(self.chips, place) * 2 + (self.core if core is None else core)

    def part(self, place, way, step, core=None):
        block = self.buf.at[self.slot(place, core)]
        if step == self.half - 1:
            block = block.at[pl.ds(way * (self.rows // 2), self.rows // 2)]
        return block

    def ring(self, way, step):
        sign = 1 - 2 * way
        block = self.part(self.place - sign * step, way, step)
        return remote(
            block,
            block,
            self.ring_send.at[way * self.half + step],
            self.ring_recv.at[way * self.half + step],
            self.slot(self.place + sign),
        )

    def side(self, index, block):
        return remote(
            block,
            block,
            self.side_send.at[index],
            self.side_recv.at[index],
            self.slot(self.place, 1 - self.core),
        )

    def go(self, copy):
        copy.start()
        self.started.append(copy)

    def start(self):
        for way in range(2):
            self.go(self.ring(way, 0))
        self.go(self.side(0, self.buf.at[self.slot(self.place)]))

    def step(self, step):
        for way in range(2):
            sign = 1 - 2 * way
            came = self.part(self.place - sign * (step + 1), way, step)
            remote(
                came,
                came,
                self.ring_send.at[way * self.half + step],
                self.ring_recv.at[way * self.half + step],
                self.slot(self.place + sign),
            ).wait_recv()
            if step + 1 < self.half:
                self.go(self.ring(way, step + 1))
            self.go(self.side(1 + 2 * step + way, came))

    def wait_side(self, step):
        if step < 0:
            block = self.buf.at[self.slot(self.place, 1 - self.core)]
            self.side(0, block).wait_recv()
            return
        for way in range(2):
            sign = 1 - 2 * way
            block = self.part(self.place - sign * (step + 1), way, step, 1 - self.core)
            self.side(1 + 2 * step + way, block).wait_recv()

    def finish(self):
        for copy in self.started:
            copy.wait_send()
        self.started = []


def kernel(
    n,
    values,
    in_b,
    out_c,
    decay_log,
    residual,
    mixer_gain,
    moe_gain,
    gates,
    w_down,
    w_in,
    w_out,
    mixed_out,
    mix_out,
    w_buf,
    lat_buf,
    *rest,
):
    chips = n // 2
    half = chips // 2
    apart = n <= 16
    if apart:
        parts, rest = rest[0], rest[1:]
    else:
        parts = lat_buf
    (
        y_buf,
        logs_t,
        normed,
        acc,
        st_send,
        st_recv,
        st_back,
        st_enter,
        gate_buf,
        win_buf,
        wout_buf,
        side_parts,
        sums,
        half_sums,
        local_sem,
        st_sem,
        st_rsem,
        back_sem,
        back_rsem,
        gate_sem,
        gate_rsem,
        w_ring_s,
        w_ring_r,
        w_side_s,
        w_side_r,
        l_ring_s,
        l_ring_r,
        l_side_s,
        l_side_r,
        p_side_s,
        p_side_r,
        s_send,
        s_recv,
    ) = rest
    me = lax.axis_index("ctx")
    core = lax.rem(me, 2)
    place = ring_place(chips, me // 2)
    tok = values.shape[0]
    width = values.shape[1] // n

    load_down = pltpu.make_async_copy(w_down, w_buf.at[me], local_sem.at[0])
    load_in = pltpu.make_async_copy(w_in.at[0], win_buf, local_sem.at[1])
    load_out = pltpu.make_async_copy(w_out.at[0], wout_buf, local_sem.at[2])
    load_down.start()
    load_in.start()
    load_out.start()

    barrier = pltpu.get_barrier_semaphore()

    @pl.loop(1, n)
    def _(i):
        pl.semaphore_signal(
            barrier, inc=1, device_id={"ctx": lax.rem(me + i, n)}, device_id_type=MESH
        )

    pl.semaphore_wait(barrier, n - 1)
    load_down.wait()
    down = Gather(w_buf, chips, place, core, (w_ring_s, w_ring_r, w_side_s, w_side_r))
    down.start()

    def gate_copy(to):
        return remote(gates.at[to], gate_buf.at[me], gate_sem.at[to], gate_rsem.at[me], to)

    @pl.loop(1, n)
    def _(i):
        gate_copy(lax.rem(me + i, n)).start()

    gate_buf[me] = gates[me]

    row = lax.broadcasted_iota(jnp.int32, (tok, tok), 0)
    col = lax.broadcasted_iota(jnp.int32, (tok, tok), 1)
    lower = row >= col
    lower_f = lower.astype(F32)
    upper_f = (row <= col).astype(F32)
    left = lax.broadcasted_iota(jnp.int32, (tok, 128), 1) < P_SIZE
    left_row = left[:1]
    extra_row = lax.broadcasted_iota(jnp.int32, (EXTRA, 128), 0)

    def pair(a, b):
        return jnp.where(left, a, b)

    def st_copy(to):
        return remote(st_send.at[to], st_recv.at[me], st_sem.at[to], st_rsem.at[me], to)

    per_gp = n // 4

    @pl.loop(0, 4)
    def _(gp):
        logs = decay_log[pl.ds(pl.multiple_of(gp * 16, 16), 16), :]
        run = jnp.dot(logs, upper_f, precision=lax.Precision.HIGHEST, preferred_element_type=F32)
        run_t = lax.dot_general(
            lower_f,
            logs,
            (((1,), (1,)), ((), ())),
            precision=lax.Precision.HIGHEST,
            preferred_element_type=F32,
        )
        logs_t[gp] = run_t
        tails = jnp.exp(run_t[tok - 1 : tok, :] - run_t)
        total = jnp.exp(run_t[tok - 1 : tok, :])
        two = pl.ds(pl.multiple_of(gp * 128, 128), 128)
        b2, c2 = in_b[:, two], out_c[:, two]
        for gi in range(2):
            b = b2[:, gi * N : (gi + 1) * N]
            c = c2[:, gi * N : (gi + 1) * N]
            scores = lax.dot_general(c, b, (((1,), (1,)), ((), ())), preferred_element_type=F32)
            for hp in range(4):
                h = gi * 8 + hp * 2
                cols = pl.ds(pl.multiple_of(gp * 1024 + gi * 512 + hp * 128, 128), 128)
                v = values[:, cols]
                weights = []
                for k in range(2):
                    spread = run_t[:, h + k : h + k + 1] - run[h + k : h + k + 1, :]
                    decays = jnp.exp(jnp.where(lower, spread, -1e30))
                    weights.append((scores * decays).astype(BF16))
                zero = jnp.zeros_like(v)
                stacked = jnp.concatenate([pair(v, zero), pair(zero, v)], axis=0)
                y_buf[:, cols] = jnp.dot(
                    jnp.concatenate(weights, axis=1), stacked, preferred_element_type=F32
                )
                tail = pair(tails[:, h : h + 1], tails[:, h + 1 : h + 2])
                scaled = (v.astype(F32) * tail).astype(BF16)
                update = lax.dot_general(
                    b, scaled, (((0,), (0,)), ((), ())), preferred_element_type=F32
                ).astype(BF16)
                dec = jnp.where(left_row, total[:, h : h + 1], total[:, h + 1 : h + 2])
                high = dec.astype(BF16).astype(F32)
                mid = (dec - high).astype(BF16).astype(F32)
                low = dec - high - mid
                extra = jnp.where(
                    extra_row == 0, high, jnp.where(extra_row == 1, mid, low)
                ).astype(BF16)
                k = gi * 4 + hp
                if width >= 128:
                    per = width // 128
                    to = gp * (8 // per) + k // per
                    at = (k % per) * 128
                    st_send[to, :N, at : at + 128] = update
                    st_send[to, N:, at : at + 128] = extra
                else:
                    per = 128 // width
                    for part in range(per):
                        to = gp * 8 * per + k * per + part
                        lanes = slice(part * width, (part + 1) * width)
                        st_send[to, :N, :] = update[:, lanes]
                        st_send[to, N:, :] = extra[:, lanes]

        @pl.loop(0, per_gp)
        def _(i):
            to = gp * per_gp + i

            @pl.when(to != me)
            def _():
                st_copy(to).start()

            @pl.when(to == me)
            def _():
                st_recv[me] = st_send[me]

    down.step(0)

    def back_copy(to):
        return remote(st_back.at[to], st_enter.at[me], back_sem.at[to], back_rsem.at[me], to)

    def advance(i, state):
        @pl.when(i != me)
        def _():
            remote(
                st_send.at[i], st_recv.at[i], st_sem.at[i], st_rsem.at[i], i
            ).wait_recv()

        block = st_recv[i].astype(F32)
        dec = block[N : N + 1] + block[N + 1 : N + 2] + block[N + 2 : N + 3]
        st_back[i] = state.astype(BF16)

        @pl.when(i != me)
        def _():
            back_copy(i).start()

        @pl.when(i == me)
        def _():
            st_enter[me] = st_back[me]

        return dec * state + block[:N]

    lax.fori_loop(0, n, advance, jnp.zeros((N, width), F32))
    if half > 1:
        down.step(1)

    @pl.loop(1, n)
    def _(i):
        src = lax.rem(me + i, n)
        remote(
            st_back.at[src], st_enter.at[src], back_sem.at[src], back_rsem.at[src], src
        ).wait_recv()

    def finish_mixer(gp, squares):
        reach_scale = jnp.exp(logs_t[gp])
        c2 = out_c[:, pl.ds(pl.multiple_of(gp * 128, 128), 128)]
        for gi in range(2):
            c = c2[:, gi * N : (gi + 1) * N]
            for hp in range(4):
                h = gi * 8 + hp * 2
                cols = pl.ds(pl.multiple_of(gp * 1024 + gi * 512 + hp * 128, 128), 128)
                k = gi * 4 + hp
                if width >= 128:
                    per = width // 128
                    at = (k % per) * 128
                    enter = st_enter[gp * (8 // per) + k // per, :, at : at + 128]
                else:
                    per = 128 // width
                    first = gp * 8 * per + k * per
                    enter = jnp.concatenate([st_enter[first + j] for j in range(per)], axis=1)
                reach = jnp.dot(c, enter, preferred_element_type=F32)
                y = y_buf[:, cols] + pair(reach_scale[:, h : h + 1], reach_scale[:, h + 1 : h + 2]) * reach
                square = y * y
                both = jnp.sum(square, axis=1, keepdims=True)
                one = jnp.sum(jnp.where(left, square, 0.0), axis=1, keepdims=True)
                other = jnp.sum(jnp.where(left, 0.0, square), axis=1, keepdims=True)
                del both
                scale = pair(
                    lax.rsqrt(one * (1.0 / P_SIZE) + 1e-05),
                    lax.rsqrt(other * (1.0 / P_SIZE) + 1e-05),
                )
                mixed = (
                    residual[:, cols].astype(F32) + y * scale * mixer_gain[:, cols]
                ).astype(BF16)
                mixed_out[:, cols] = mixed
                wide = mixed.astype(F32)
                squares = squares + wide * wide
        return squares

    squares = lax.fori_loop(0, 4, finish_mixer, jnp.zeros((tok, 128), F32))
    mean = jnp.sum(squares, axis=1, keepdims=True) * (1.0 / (n * width))
    row_scale = lax.rsqrt(mean + 1e-05)
    rows = w_buf.shape[1]
    if rows >= 128:

        @pl.loop(0, n)
        def _(i):
            cols = pl.ds(pl.multiple_of(i * rows, rows), rows)
            wide = mixed_out[:, cols].astype(F32)
            normed[i] = (wide * row_scale * moe_gain[:, cols]).astype(BF16)
    else:

        @pl.loop(0, n // 2)
        def _(i):
            cols = pl.ds(pl.multiple_of(i * 128, 128), 128)
            wide = mixed_out[:, cols].astype(F32)
            both = (wide * row_scale * moe_gain[:, cols]).astype(BF16)
            normed[2 * i] = both[:, :rows]
            normed[2 * i + 1] = both[:, rows:]

    for step in range(2, half):
        down.step(step)
    for step in range(-1, half):
        down.wait_side(step)
    acc[...] = jnp.zeros_like(acc)

    @pl.loop(0, n)
    def _(i):
        acc[...] += jnp.dot(normed[i], w_buf[i], preferred_element_type=F32)

    lat_buf[me] = acc[...].astype(BF16)

    lat = Gather(lat_buf, chips, place, core, (l_ring_s, l_ring_r, l_side_s, l_side_r))
    lat.start()

    @pl.loop(1, n)
    def _(i):
        src = lax.rem(me + i, n)
        remote(
            gates.at[src], gate_buf.at[src], gate_sem.at[src], gate_rsem.at[src], src
        ).wait_recv()

    load_in.wait()
    load_out.wait()

    def expert(place_of):
        chip = ring_chip(chips, place_of)
        x = lat_buf[pl.ds(2 * chip, 2)].reshape(2 * tok, lat_buf.shape[2])
        hidden = jnp.dot(x, win_buf[...], preferred_element_type=F32)
        hidden = jnp.square(jnp.maximum(hidden, 0.0)).astype(BF16)
        out = jnp.dot(hidden, wout_buf[...], preferred_element_type=F32).astype(BF16).astype(F32)
        for k in range(2):
            gate = jnp.transpose(gate_buf[2 * chip + k])[:, :1]
            parts[2 * chip + k] = (out[k * tok : (k + 1) * tok] * gate).astype(BF16)

    def part_copy(index, place_of):
        chip = ring_chip(chips, place_of)
        return remote(
            parts.at[2 * chip + 1 - core],
            side_parts.at[chip],
            p_side_s.at[index],
            p_side_r.at[index],
            ring_chip(chips, place) * 2 + 1 - core,
        )

    def work(step):
        if step < 0:
            expert(place)
            part_copy(0, place).start()
        elif step == half - 1:
            expert(place + half)
            part_copy(2 * half - 1, place + half).start()
        else:

            @pl.loop(0, 2)
            def _(way):
                there = place - (1 - 2 * way) * (step + 1)
                expert(there)
                part_copy(1 + 2 * step + way, there).start()

    if apart:
        for step in range(half):
            lat.step(step)
            lat.wait_side(step - 1)
            work(step - 1)
        lat.wait_side(half - 1)
        work(half - 1)
        lat.finish()
    else:
        for step in range(half):
            lat.step(step)
        for step in range(-1, half):
            lat.wait_side(step)
        lat.finish()
        for step in range(-1, half):
            work(step)

    def pair_sum(index, place_of):
        chip = ring_chip(chips, place_of)
        part_copy(index, place_of).wait_recv()
        slot = 2 * chip + core
        parts[slot] = (parts[slot].astype(F32) + side_parts[chip].astype(F32)).astype(BF16)

    cut = tok // 2

    def sum_copy(way, step):
        sign = 1 - 2 * way
        there = place + sign * (half - step)
        block = parts.at[2 * ring_chip(chips, there) + core]
        to = ring_chip(chips, place + sign) * 2 + core
        if step == 0:
            block = block.at[pl.ds(way * cut, cut)]
            target = half_sums.at[way]
        else:
            target = sums.at[way * (half - 1) + step - 1]
        sem = way * half + step
        return remote(block, target, s_send.at[sem], s_recv.at[sem], to)

    sent = []
    pair_sum(2 * half - 1, place + half)
    for way in range(2):
        sent.append(sum_copy(way, 0))
        sent[-1].start()
    for step in range(1, half):
        for way in range(2):
            there = place + (1 - 2 * way) * (half - step)
            pair_sum(1 + 2 * (half - step - 1) + (1 - way), there)
        for way in range(2):
            there = place + (1 - 2 * way) * (half - step)
            slot = 2 * ring_chip(chips, there) + core
            sum_copy(way, step - 1).wait_recv()
            if step == 1:
                some = pl.ds(way * cut, cut)
                parts[slot, some] = (
                    parts[slot, some].astype(F32) + half_sums[way].astype(F32)
                ).astype(BF16)
            else:
                parts[slot] = (
                    parts[slot].astype(F32)
                    + sums[way * (half - 1) + step - 2].astype(F32)
                ).astype(BF16)
            sent.append(sum_copy(way, step))
            sent[-1].start()
    part_copy(0, place).wait_recv()
    mine = ring_chip(chips, place)
    whole = parts[2 * mine + core].astype(F32) + side_parts[mine].astype(F32)
    for way in range(2):
        sum_copy(way, half - 1).wait_recv()
        whole = whole + sums[way * (half - 1) + half - 2].astype(F32)
    mix_out[...] = whole.astype(BF16)

    for copy in sent:
        copy.wait_send()
    for index in range(2 * half):
        part_copy(index, place).wait_send()
    down.finish()

    @pl.loop(1, n)
    def _(i):
        to = lax.rem(me + i, n)
        st_copy(to).wait_send()
        back_copy(to).wait_send()
        gate_copy(to).wait_send()


def on_device(
    values,
    in_b,
    out_c,
    decay_log,
    residual,
    mixer_gain,
    moe_gain,
    w_down,
    w_in,
    w_out,
    routes,
    gate_int,
):
    n = lax.axis_size("ctx")
    tok, width = values.shape
    latent = w_down.shape[1]
    chips = n // 2
    half = chips // 2
    gate_float = gate_int.astype(F32)
    gate = gate_float / jnp.sum(gate_float, axis=1, keepdims=True)
    named = routes[None] == jnp.arange(n, dtype=jnp.int32)[:, None, None]
    table = jnp.sum(jnp.where(named, gate[None], 0.0), axis=2)
    gates = jnp.broadcast_to(table[:, None, :], (n, 8, tok))
    vmem = pl.BlockSpec(memory_space=pltpu.VMEM)
    anywhere = pl.BlockSpec(memory_space=pl.ANY)
    dma = lambda count: pltpu.SemaphoreType.DMA((count,))
    share = width // n
    scratch = [
        pltpu.VMEM((n,) + w_down.shape, BF16),
        pltpu.VMEM((n, tok, latent), BF16),
    ]
    if n <= 16:
        scratch.append(pltpu.VMEM((n, tok, latent), BF16))
    scratch += [
        pltpu.VMEM((tok, width), F32),
        pltpu.VMEM((4, tok, 16), F32),
        pltpu.VMEM((n, tok, w_down.shape[0]), BF16),
        pltpu.VMEM((tok, latent), F32),
        pltpu.VMEM((n, N + EXTRA, share), BF16),
        pltpu.VMEM((n, N + EXTRA, share), BF16),
        pltpu.VMEM((n, N, share), BF16),
        pltpu.VMEM((n, N, share), BF16),
        pltpu.VMEM((n, 8, tok), F32),
        pltpu.VMEM(w_in.shape[1:], BF16),
        pltpu.VMEM(w_out.shape[1:], BF16),
        pltpu.VMEM((chips, tok, latent), BF16),
        pltpu.VMEM((2 * (half - 1), tok, latent), BF16),
        pltpu.VMEM((2, tok // 2, latent), BF16),
        dma(3),
    ]
    scratch += [dma(n)] * 6
    scratch += [dma(2 * half), dma(2 * half), dma(2 * half + 1), dma(2 * half + 1)] * 2
    scratch += [dma(2 * half)] * 4
    return pl.pallas_call(
        functools.partial(kernel, n),
        out_shape=(
            jax.ShapeDtypeStruct((tok, width), BF16),
            jax.ShapeDtypeStruct((tok, latent), BF16),
        ),
        in_specs=[vmem] * 8 + [anywhere] * 3,
        out_specs=(vmem, vmem),
        scratch_shapes=scratch,
        compiler_params=pltpu.CompilerParams(
            collective_id=0, has_side_effects=True, vmem_limit_bytes=62 * 1024 * 1024
        ),
    )(
        values,
        in_b,
        out_c,
        decay_log,
        residual,
        mixer_gain.reshape(1, -1),
        moe_gain.reshape(1, -1),
        gates,
        w_down,
        w_in,
        w_out,
    )


def solution(mesh):
    return jax.shard_map(
        on_device,
        mesh=mesh,
        in_specs=(
            P(("groups", "ctx"), None),
            P(("groups", "ctx"), None),
            P(("groups", "ctx"), None),
            P(None, ("groups", "ctx")),
            P(("groups", "ctx"), None),
            P(),
            P(),
            P("ctx", None),
            P("ctx", None, None),
            P("ctx", None, None),
            P(("groups", "ctx"), None),
            P(("groups", "ctx"), None),
        ),
        out_specs=(P(("groups", "ctx"), None), P(("groups", "ctx"), None)),
        check_vma=False,
    )
```

time: 430 us -> 149 us (0.35); the launches traced: 423 us -> 148 us
  waiting for transfers between devices: 188 us -> 0 us
  Pallas kernels: 0 us -> 142 us
  blocking collectives: 82.3 us -> 0 us
  other arithmetic: 75.8 us -> 2.1 us
  local copies, waits for them, and re-layouts: 34 us -> 3.67 us
  matrix products: 23.9 us -> 0 us
  between operations: 14.2 us -> 0.65 us
  starting transfers between devices: 4.65 us -> 0 us
    all_gather x2 -> x0, waiting for transfers between devices: 143 us -> none  [the longest x1 132 us: prefix(): everything = jax.tree.map(lambda part: lax.all_gather(part, axis), array)]
    pallas_call x0 -> x1, Pallas kernels: none -> 142 us  [on_device(): pl.pallas_call(functools.partial(kernel, n), out_shape=(jax.ShapeDtypeStr...]
    select_n x17 -> x0, other arithmetic: 61.9 us -> none  [the longest x16 61.2 us: step(): return jax.tree.map(lambda a, b: jnp.where(reached, a, b), new, before)]
    all_to_all x1 -> x0, blocking collectives: 58.4 us -> none  [on_device(): lax.all_to_all(outgoing, 'ctx', split_axis=0, concat_axis=0, tiled=True)]
    all_to_all x1 -> x0, waiting for transfers between devices: 44.2 us -> none  [on_device(): lax.all_to_all(produced.reshape(devices * local_count, slot_count, L), 'c...]
    all_gather x1 -> x0, blocking collectives: 23.9 us -> none  [prefix(): everything = jax.tree.map(lambda part: lax.all_gather(part, axis), array)]
    dot_general x6 -> x0, matrix products: 23.9 us -> none  [the longest x1 8.82 us: on_device(): jnp.einsum('jecf,efl->jecl', hidden_act, w_out, preferred_element_type=jn...]
    scatter x1 -> x0, local copies, waits for them, and re-layouts: 8.09 us -> none  [on_device(): outgoing = jnp.zeros((experts * capacity, L), jnp.bfloat16).at[targets].s...]
  transfers between devices with their start and end apart: 3 -> 0, of which waited for: 3 -> 0; matrix products, arithmetic and copies ran while one was open for 20% -> 0% of each run, Pallas kernels for 0% -> 0%
where the time goes in v1:
time: 149 us; the launch traced here: 148 us
  Pallas kernels  142 us (95%)
  local copies, waits for them, and re-layouts  3.67 us (2%)
  other arithmetic  2.1 us (1%)
    pallas_call x1, Pallas kernels, on_device(): pl.pallas_call(functools.partial(kernel, n), out_shape=(jax.ShapeDtypeStr...  142 us
    unnamed x4, local copies, waits for them, and re-layouts  3.04 us

profile of v1, /device:TPU:0, one launch (start us, length us, event | category | flops | bytes accessed | tf_op | source)
XLA Modules:
  0.0 148.4 jit_solution(14651681942097157248)
XLA Ops:
  0.6 0.7 convert_reduce_fusion
  1.3 0.7 convert_divide_fusion
  2.0 0.7 select_reduce_fusion
  2.7 0.6 broadcast_in_dim.24.gates
  3.4 142.0 %shard_map.131 = (bf16[128,4096]{1,0:T(8,128)(2,1)}, bf16[128,1024]{1,0:T(8,128)(2,1)}) custom-call(bf16[128,4096]{1,0:T(8,128)(2,1)} %values.1, bf16[128,512]{1,0:T(8,128)(2,1)} %in_b.1, bf16[128,512]{1,0:T(8,128)(2,1)} %out_c.1, f32[64,128]{1,0:T(8,128)} %decay_log.1, bf16[128,4096]{1,0:T(8,128)(2,1)} %residual.1, f32[1,4096]{1,0:T(1,128)} %bitcast.2, ...), custom_call_target="tpu_custom_call" | custom-call | tf_op jit(solution)/shard_map/pallas_call | solution.py:601
  145.4 0.0 copy-start
  145.4 2.3 %copy.18 = bf16[128,4096]{1,0:T(8,128)(2,1)} copy(bf16[128,4096]{1,0:T(8,128)(2,1)} %get-tuple-element.4) | data formatting | bytes 2097152
  147.7 0.0 copy-done
  147.7 0.7 copy.19
Async XLA Ops:
  145.4 2.3 %copy-start = (bf16[128,1024]{1,0:T(8,128)(2,1)S(1)}, bf16[128,1024]{1,0:T(8,128)(2,1)}, u32[]{:S(2)}) copy-start(bf16[128,1024]{1,0:T(8,128)(2,1)} %get-tuple-element.5) | copy-start | bytes 786436

commit v2 on v1

--- a/solution.py
+++ b/solution.py
@@ -43,31 +43,37 @@
 
 
 class Gather:
-    def __init__(self, buf, chips, place, core, sems):
+    def __init__(self, buf, chips, place, core, sems, skip=0, parity=0, partner=0):
         self.buf, self.chips, self.place, self.core = buf, chips, place, core
         self.half = chips // 2
         self.rows = buf.shape[1]
-        self.ring_send, self.ring_recv, self.side_send, self.side_recv = sems
+        self.skip, self.parity, self.partner = skip, parity, partner
+        self.piece = (self.rows - skip) // 2
+        self.ring_send, self.ring_recv, self.side_send, self.side_recv = sems[:4]
+        self.cross = sems[4:]
         self.started = []
 
     def slot(self, place, core=None):
         return ring_chip(self.chips, place) * 2 + (self.core if core is None else core)
 
-    def part(self, place, way, step, core=None):
-        block = self.buf.at[self.slot(place, core)]
-        if step == self.half - 1:
-            block = block.at[pl.ds(way * (self.rows // 2), self.rows // 2)]
-        return block
-
-    def ring(self, way, step):
+    def rows_at(self, place, start, count, core=None):
+        return self.buf.at[self.slot(place, core), pl.ds(pl.multiple_of(start, 16), count)]
+
+    def part(self, place, piece, core=None):
+        return self.rows_at(place, self.parity * self.skip + piece * self.piece, self.piece, core)
+
+    def pieces(self, way, step):
+        return (way,) if step == self.half - 1 else (way, 1 - way)
+
+    def index(self, way, step, piece):
+        return (way * self.half + step) * 2 + piece
+
+    def ring(self, way, step, piece):
         sign = 1 - 2 * way
-        block = self.part(self.place - sign * step, way, step)
+        block = self.part(self.place - sign * (step + 1), piece)
+        sem = self.index(way, step, piece)
         return remote(
-            block,
-            block,
-            self.ring_send.at[way * self.half + step],
-            self.ring_recv.at[way * self.half + step],
-            self.slot(self.place + sign),
+            block, block, self.ring_send.at[sem], self.ring_recv.at[sem], self.slot(self.place + sign)
         )
 
     def side(self, index, block):
@@ -83,35 +89,84 @@
         copy.start()
         self.started.append(copy)
 
+    def send(self, way, step, piece):
+        sign = 1 - 2 * way
+        block = self.part(self.place - sign * step, piece)
+        sem = self.index(way, step, piece)
+        self.go(
+            remote(
+                block,
+                block,
+                self.ring_send.at[sem],
+                self.ring_recv.at[sem],
+                self.slot(self.place + sign),
+            )
+        )
+
     def start(self):
-        for way in range(2):
-            self.go(self.ring(way, 0))
+        for k in range(2):
+            for way in range(2):
+                self.send(way, 0, self.pieces(way, 0)[k])
         self.go(self.side(0, self.buf.at[self.slot(self.place)]))
 
+    def far(self, step):
+        if step == self.half - 1:
+            return ((2 * step, self.place + self.half),)
+        return tuple((2 * step + way, self.place - (1 - 2 * way) * (step + 1)) for way in range(2))
+
+    def crossing(self, index, place, mine, core=None):
+        start = (self.parity if mine else 1 - self.parity) * (self.rows - self.skip)
+        block = self.rows_at(place, start, self.skip, core)
+        if core is None:
+            return pltpu.make_async_remote_copy(
+                src_ref=block,
+                dst_ref=block,
+                send_sem=self.cross[0].at[index],
+                recv_sem=self.cross[1].at[index],
+                device_id={"groups": self.partner},
+                device_id_type=MESH,
+            )
+        return remote(
+            block,
+            block,
+            self.cross[2].at[index],
+            self.cross[3].at[index],
+            self.slot(self.place, 1 - self.core),
+        )
+
     def step(self, step):
-        for way in range(2):
-            sign = 1 - 2 * way
-            came = self.part(self.place - sign * (step + 1), way, step)
-            remote(
-                came,
-                came,
-                self.ring_send.at[way * self.half + step],
-                self.ring_recv.at[way * self.half + step],
-                self.slot(self.place + sign),
-            ).wait_recv()
-            if step + 1 < self.half:
-                self.go(self.ring(way, step + 1))
-            self.go(self.side(1 + 2 * step + way, came))
+        for k in range(len(self.pieces(0, step))):
+            for way in range(2):
+                piece = self.pieces(way, step)[k]
+                self.ring(way, step, piece).wait_recv()
+                if step + 1 < self.half and piece in self.pieces(way, step + 1):
+                    self.send(way, step + 1, piece)
+                sign = 1 - 2 * way
+                came = self.part(self.place - sign * (step + 1), piece)
+                self.go(self.side(1 + self.index(way, step, piece), came))
+        if self.skip:
+            for index, place in self.far(step):
+                self.go(self.crossing(index, place, True))
+            if step:
+                self.cross_step(step - 1)
+
+    def cross_step(self, step):
+        for index, place in self.far(step):
+            self.crossing(index, place, False).wait_recv()
+            self.go(self.crossing(index, place, False, self.core))
 
     def wait_side(self, step):
+        other = 1 - self.core
         if step < 0:
-            block = self.buf.at[self.slot(self.place, 1 - self.core)]
-            self.side(0, block).wait_recv()
+            self.side(0, self.buf.at[self.slot(self.place, other)]).wait_recv()
             return
         for way in range(2):
-            sign = 1 - 2 * way
-            block = self.part(self.place - sign * (step + 1), way, step, 1 - self.core)
-            self.side(1 + 2 * step + way, block).wait_recv()
+            for piece in self.pieces(way, step):
+                block = self.part(self.place - (1 - 2 * way) * (step + 1), piece, other)
+                self.side(1 + self.index(way, step, piece), block).wait_recv()
+        if self.skip:
+            for index, place in self.far(step):
+                self.crossing(index, place, False, other).wait_recv()
 
     def finish(self):
         for copy in self.started:
@@ -121,6 +176,7 @@
 
 def kernel(
     n,
+    skip,
     values,
     in_b,
     out_c,
@@ -154,6 +210,10 @@
         st_recv,
         st_back,
         st_enter,
+        before,
+        tot_send,
+        tot_recv,
+        carry,
         gate_buf,
         win_buf,
         wout_buf,
@@ -165,12 +225,18 @@
         st_rsem,
         back_sem,
         back_rsem,
+        tot_sem,
+        tot_rsem,
         gate_sem,
         gate_rsem,
         w_ring_s,
         w_ring_r,
         w_side_s,
         w_side_r,
+        x_send,
+        x_recv,
+        x_side_s,
+        x_side_r,
         l_ring_s,
         l_ring_r,
         l_side_s,
@@ -201,9 +267,25 @@
             barrier, inc=1, device_id={"ctx": lax.rem(me + i, n)}, device_id_type=MESH
         )
 
-    pl.semaphore_wait(barrier, n - 1)
+    group = lax.axis_index("groups")
+    parity = lax.rem(group, 2)
+    partner = group + 1 - 2 * parity
+    if skip:
+        pl.semaphore_signal(
+            barrier, inc=1, device_id={"groups": partner}, device_id_type=MESH
+        )
+    pl.semaphore_wait(barrier, n if skip else n - 1)
     load_down.wait()
-    down = Gather(w_buf, chips, place, core, (w_ring_s, w_ring_r, w_side_s, w_side_r))
+    down = Gather(
+        w_buf,
+        chips,
+        place,
+        core,
+        (w_ring_s, w_ring_r, w_side_s, w_side_r, x_send, x_recv, x_side_s, x_side_r),
+        skip,
+        parity,
+        partner,
+    )
     down.start()
 
     def gate_copy(to):
@@ -227,10 +309,13 @@
     def pair(a, b):
         return jnp.where(left, a, b)
 
+    plane, quarter = me // 4, lax.rem(me, 4)
+    planes = n // 4
+
     def st_copy(to):
-        return remote(st_send.at[to], st_recv.at[me], st_sem.at[to], st_rsem.at[me], to)
-
-    per_gp = n // 4
+        return remote(
+            st_send.at[to], st_recv.at[quarter], st_sem.at[to], st_rsem.at[quarter], plane * 4 + to
+        )
 
     @pl.loop(0, 4)
     def _(gp):
@@ -278,68 +363,97 @@
                 extra = jnp.where(
                     extra_row == 0, high, jnp.where(extra_row == 1, mid, low)
                 ).astype(BF16)
-                k = gi * 4 + hp
-                if width >= 128:
-                    per = width // 128
-                    to = gp * (8 // per) + k // per
-                    at = (k % per) * 128
-                    st_send[to, :N, at : at + 128] = update
-                    st_send[to, N:, at : at + 128] = extra
-                else:
-                    per = 128 // width
-                    for part in range(per):
-                        to = gp * 8 * per + k * per + part
-                        lanes = slice(part * width, (part + 1) * width)
-                        st_send[to, :N, :] = update[:, lanes]
-                        st_send[to, N:, :] = extra[:, lanes]
-
-        @pl.loop(0, per_gp)
-        def _(i):
-            to = gp * per_gp + i
-
-            @pl.when(to != me)
-            def _():
-                st_copy(to).start()
-
-            @pl.when(to == me)
-            def _():
-                st_recv[me] = st_send[me]
-
-    down.step(0)
-
-    def back_copy(to):
-        return remote(st_back.at[to], st_enter.at[me], back_sem.at[to], back_rsem.at[me], to)
-
-    def advance(i, state):
-        @pl.when(i != me)
+                at = gi * 512 + hp * 128
+                st_send[gp, :N, at : at + 128] = update
+                st_send[gp, N:, at : at + 128] = extra
+
+        @pl.when(gp != quarter)
+        def _():
+            st_copy(gp).start()
+
+        @pl.when(gp == quarter)
+        def _():
+            st_recv[quarter] = st_send[quarter]
+
+    def take(block):
+        block = block.astype(F32)
+        return block[N : N + 1] + block[N + 1 : N + 2] + block[N + 2 : N + 3], block[:N]
+
+    state = jnp.zeros((N, 1024), F32)
+    total = jnp.ones((1, 1024), F32)
+    for i in range(4):
+
+        @pl.when(quarter != i)
         def _():
             remote(
-                st_send.at[i], st_recv.at[i], st_sem.at[i], st_rsem.at[i], i
+                st_send.at[i], st_recv.at[i], st_sem.at[i], st_rsem.at[i], plane * 4 + i
             ).wait_recv()
 
-        block = st_recv[i].astype(F32)
-        dec = block[N : N + 1] + block[N + 1 : N + 2] + block[N + 2 : N + 3]
-        st_back[i] = state.astype(BF16)
-
-        @pl.when(i != me)
+        before[i, :N] = state
+        before[i, N : N + 8] = jnp.broadcast_to(total, (8, 1024))
+        dec, update = take(st_recv[i])
+        state = dec * state + update
+        total = dec * total
+    high = total.astype(BF16).astype(F32)
+    mid = (total - high).astype(BF16).astype(F32)
+    place_row = lax.broadcasted_iota(jnp.int32, (EXTRA, 1024), 0)
+    tot_send[:N] = state.astype(BF16)
+    tot_send[N:] = jnp.where(
+        place_row == 0, high, jnp.where(place_row == 1, mid, total - high - mid)
+    ).astype(BF16)
+
+    def tot_copy(to):
+        return remote(
+            tot_send, tot_recv.at[plane], tot_sem.at[to], tot_rsem.at[plane], to * 4 + quarter
+        )
+
+    @pl.loop(0, planes)
+    def _(to):
+        @pl.when(to > plane)
+        def _():
+            tot_copy(to).start()
+
+    down.step(0)
+    carry[...] = jnp.zeros_like(carry)
+
+    @pl.loop(0, planes)
+    def _(i):
+        @pl.when(i < plane)
+        def _():
+            remote(
+                tot_send, tot_recv.at[i], tot_sem.at[i], tot_rsem.at[i], i * 4 + quarter
+            ).wait_recv()
+            dec, update = take(tot_recv[i])
+            carry[...] = dec * carry[...] + update
+
+    def back_copy(to):
+        return remote(
+            st_back.at[to], st_enter.at[quarter], back_sem.at[to], back_rsem.at[quarter], plane * 4 + to
+        )
+
+    for i in range(4):
+        st_back[i] = (before[i, :N] + before[i, N : N + 1] * carry[...]).astype(BF16)
+
+        @pl.when(quarter != i)
         def _():
             back_copy(i).start()
 
-        @pl.when(i == me)
+        @pl.when(quarter == i)
         def _():
-            st_enter[me] = st_back[me]
-
-        return dec * state + block[:N]
-
-    lax.fori_loop(0, n, advance, jnp.zeros((N, width), F32))
-    if half > 1:
-        down.step(1)
-
-    @pl.loop(1, n)
+            st_enter[quarter] = st_back[quarter]
+
+    for step in range(1, half - 1):
+        down.step(step)
+
+    @pl.loop(1, 4)
     def _(i):
-        src = lax.rem(me + i, n)
+        src = lax.rem(quarter + i, 4)
         remote(
-            st_back.at[src], st_enter.at[src], back_sem.at[src], back_rsem.at[src], src
+            st_back.at[src],
+            st_enter.at[src],
+            back_sem.at[src],
+            back_rsem.at[src],
+            plane * 4 + src,
         ).wait_recv()
 
     def finish_mixer(gp, squares):
@@ -350,15 +464,8 @@
             for hp in range(4):
                 h = gi * 8 + hp * 2
                 cols = pl.ds(pl.multiple_of(gp * 1024 + gi * 512 + hp * 128, 128), 128)
-                k = gi * 4 + hp
-                if width >= 128:
-                    per = width // 128
-                    at = (k % per) * 128
-                    enter = st_enter[gp * (8 // per) + k // per, :, at : at + 128]
-                else:
-                    per = 128 // width
-                    first = gp * 8 * per + k * per
-                    enter = jnp.concatenate([st_enter[first + j] for j in range(per)], axis=1)
+                at = gi * 512 + hp * 128
+                enter = st_enter[gp, :, at : at + 128]
                 reach = jnp.dot(c, enter, preferred_element_type=F32)
                 y = y_buf[:, cols] + pair(reach_scale[:, h : h + 1], reach_scale[:, h + 1 : h + 2]) * reach
                 square = y * y
@@ -399,8 +506,10 @@
             normed[2 * i] = both[:, :rows]
             normed[2 * i + 1] = both[:, rows:]
 
-    for step in range(2, half):
+    for step in range(half - 1, half):
         down.step(step)
+    if skip:
+        down.cross_step(half - 1)
     for step in range(-1, half):
         down.wait_side(step)
     acc[...] = jnp.zeros_like(acc)
@@ -484,49 +593,54 @@
 
     cut = tok // 2
 
-    def sum_copy(way, step):
+    def sum_copy(way, step, piece):
         sign = 1 - 2 * way
         there = place + sign * (half - step)
-        block = parts.at[2 * ring_chip(chips, there) + core]
+        some = pl.ds(piece * cut, cut)
+        block = parts.at[2 * ring_chip(chips, there) + core, some]
         to = ring_chip(chips, place + sign) * 2 + core
         if step == 0:
-            block = block.at[pl.ds(way * cut, cut)]
             target = half_sums.at[way]
         else:
-            target = sums.at[way * (half - 1) + step - 1]
-        sem = way * half + step
+            target = sums.at[way * (half - 1) + step - 1, some]
+        sem = (way * half + step) * 2 + piece
         return remote(block, target, s_send.at[sem], s_recv.at[sem], to)
 
     sent = []
+
+    def send_sum(way, step, piece):
+        sent.append(sum_copy(way, step, piece))
+        sent[-1].start()
+
     pair_sum(2 * half - 1, place + half)
     for way in range(2):
-        sent.append(sum_copy(way, 0))
-        sent[-1].start()
+        send_sum(way, 0, way)
     for step in range(1, half):
         for way in range(2):
             there = place + (1 - 2 * way) * (half - step)
             pair_sum(1 + 2 * (half - step - 1) + (1 - way), there)
-        for way in range(2):
-            there = place + (1 - 2 * way) * (half - step)
-            slot = 2 * ring_chip(chips, there) + core
-            sum_copy(way, step - 1).wait_recv()
-            if step == 1:
-                some = pl.ds(way * cut, cut)
-                parts[slot, some] = (
-                    parts[slot, some].astype(F32) + half_sums[way].astype(F32)
-                ).astype(BF16)
-            else:
-                parts[slot] = (
-                    parts[slot].astype(F32)
-                    + sums[way * (half - 1) + step - 2].astype(F32)
-                ).astype(BF16)
-            sent.append(sum_copy(way, step))
-            sent[-1].start()
+        for first in (True, False):
+            for way in range(2):
+                piece = 1 - way if first else way
+                there = place + (1 - 2 * way) * (half - step)
+                slot = 2 * ring_chip(chips, there) + core
+                some = pl.ds(piece * cut, cut)
+                if step > 1 or not first:
+                    sum_copy(way, step - 1, piece).wait_recv()
+                    if step == 1:
+                        came = half_sums[way]
+                    else:
+                        came = sums[way * (half - 1) + step - 2, some]
+                    parts[slot, some] = (
+                        parts[slot, some].astype(F32) + came.astype(F32)
+                    ).astype(BF16)
+                send_sum(way, step, piece)
     part_copy(0, place).wait_recv()
     mine = ring_chip(chips, place)
     whole = parts[2 * mine + core].astype(F32) + side_parts[mine].astype(F32)
     for way in range(2):
-        sum_copy(way, half - 1).wait_recv()
+        for piece in range(2):
+            sum_copy(way, half - 1, piece).wait_recv()
         whole = whole + sums[way * (half - 1) + half - 2].astype(F32)
     mix_out[...] = whole.astype(BF16)
 
@@ -539,9 +653,19 @@
     @pl.loop(1, n)
     def _(i):
         to = lax.rem(me + i, n)
+        gate_copy(to).wait_send()
+
+    @pl.loop(1, 4)
+    def _(i):
+        to = lax.rem(quarter + i, 4)
         st_copy(to).wait_send()
         back_copy(to).wait_send()
-        gate_copy(to).wait_send()
+
+    @pl.loop(0, planes)
+    def _(to):
+        @pl.when(to > plane)
+        def _():
+            tot_copy(to).wait_send()
 
 
 def on_device(
@@ -571,7 +695,6 @@
     vmem = pl.BlockSpec(memory_space=pltpu.VMEM)
     anywhere = pl.BlockSpec(memory_space=pl.ANY)
     dma = lambda count: pltpu.SemaphoreType.DMA((count,))
-    share = width // n
     scratch = [
         pltpu.VMEM((n,) + w_down.shape, BF16),
         pltpu.VMEM((n, tok, latent), BF16),
@@ -583,10 +706,14 @@
         pltpu.VMEM((4, tok, 16), F32),
         pltpu.VMEM((n, tok, w_down.shape[0]), BF16),
         pltpu.VMEM((tok, latent), F32),
-        pltpu.VMEM((n, N + EXTRA, share), BF16),
-        pltpu.VMEM((n, N + EXTRA, share), BF16),
-        pltpu.VMEM((n, N, share), BF16),
-        pltpu.VMEM((n, N, share), BF16),
+        pltpu.VMEM((4, N + EXTRA, 1024), BF16),
+        pltpu.VMEM((4, N + EXTRA, 1024), BF16),
+        pltpu.VMEM((4, N, 1024), BF16),
+        pltpu.VMEM((4, N, 1024), BF16),
+        pltpu.VMEM((4, N + 8, 1024), F32),
+        pltpu.VMEM((N + EXTRA, 1024), BF16),
+        pltpu.VMEM((n // 4, N + EXTRA, 1024), BF16),
+        pltpu.VMEM((N, 1024), F32),
         pltpu.VMEM((n, 8, tok), F32),
         pltpu.VMEM(w_in.shape[1:], BF16),
         pltpu.VMEM(w_out.shape[1:], BF16),
@@ -595,11 +722,13 @@
         pltpu.VMEM((2, tok // 2, latent), BF16),
         dma(3),
     ]
-    scratch += [dma(n)] * 6
-    scratch += [dma(2 * half), dma(2 * half), dma(2 * half + 1), dma(2 * half + 1)] * 2
-    scratch += [dma(2 * half)] * 4
+    scratch += [dma(4)] * 4 + [dma(n // 4)] * 2 + [dma(n)] * 2
+    ring = [dma(4 * half)] * 2 + [dma(4 * half + 1)] * 2
+    scratch += ring + [dma(2 * half)] * 4 + ring
+    scratch += [dma(2 * half)] * 2 + [dma(4 * half)] * 2
+    skip = w_down.shape[0] // 4 // 32 * 32 if lax.axis_size("groups") % 2 == 0 else 0
     return pl.pallas_call(
-        functools.partial(kernel, n),
+        functools.partial(kernel, n, skip),
         out_shape=(
             jax.ShapeDtypeStruct((tok, width), BF16),
             jax.ShapeDtypeStruct((tok, latent), BF16),

time: 149 us -> 128 us (0.86)
  Pallas kernels: 142 us -> 121 us
    pallas_call x1, Pallas kernels: 142 us -> 121 us  [on_device(): pl.pallas_call(functools.partial(kernel, n, skip), out_shape=(jax.ShapeDt...]
where the time goes in v2:
time: 128 us; the launch traced here: 127 us
  Pallas kernels  121 us (95%)
  local copies, waits for them, and re-layouts  3.67 us (3%)
  other arithmetic  2.1 us (2%)
    pallas_call x1, Pallas kernels, on_device(): pl.pallas_call(functools.partial(kernel, n, skip), out_shape=(jax.ShapeDt...  121 us
    unnamed x4, local copies, waits for them, and re-layouts  3.04 us

profile of v2, /device:TPU:0, one launch (start us, length us, event | category | flops | bytes accessed | tf_op | source)
XLA Modules:
  0.0 127.5 jit_solution(4093999628820133907)
XLA Ops:
  0.6 0.7 convert_reduce_fusion
  1.3 0.7 convert_divide_fusion
  2.0 0.7 select_reduce_fusion
  2.7 0.6 broadcast_in_dim.24.gates
  3.4 121.0 %shard_map.131 = (bf16[128,4096]{1,0:T(8,128)(2,1)}, bf16[128,1024]{1,0:T(8,128)(2,1)}) custom-call(bf16[128,4096]{1,0:T(8,128)(2,1)} %values.1, bf16[128,512]{1,0:T(8,128)(2,1)} %in_b.1, bf16[128,512]{1,0:T(8,128)(2,1)} %out_c.1, f32[64,128]{1,0:T(8,128)} %decay_log.1, bf16[128,4096]{1,0:T(8,128)(2,1)} %residual.1, f32[1,4096]{1,0:T(1,128)} %bitcast.2, ...), custom_call_target="tpu_custom_call" | custom-call | tf_op jit(solution)/shard_map/pallas_call | solution.py:730
  124.4 0.0 copy-start
  124.4 2.3 %copy.18 = bf16[128,4096]{1,0:T(8,128)(2,1)} copy(bf16[128,4096]{1,0:T(8,128)(2,1)} %get-tuple-element.4) | data formatting | bytes 2097152
  126.7 0.0 copy-done
  126.8 0.7 copy.19
Async XLA Ops:
  124.4 2.3 %copy-start = (bf16[128,1024]{1,0:T(8,128)(2,1)S(1)}, bf16[128,1024]{1,0:T(8,128)(2,1)}, u32[]{:S(2)}) copy-start(bf16[128,1024]{1,0:T(8,128)(2,1)} %get-tuple-element.5) | copy-start | bytes 786436

commit v3 on v2

--- a/solution.py
+++ b/solution.py
@@ -291,12 +291,6 @@
     def gate_copy(to):
         return remote(gates.at[to], gate_buf.at[me], gate_sem.at[to], gate_rsem.at[me], to)
 
-    @pl.loop(1, n)
-    def _(i):
-        gate_copy(lax.rem(me + i, n)).start()
-
-    gate_buf[me] = gates[me]
-
     row = lax.broadcasted_iota(jnp.int32, (tok, tok), 0)
     col = lax.broadcasted_iota(jnp.int32, (tok, tok), 1)
     lower = row >= col
@@ -414,6 +408,13 @@
             tot_copy(to).start()
 
     down.step(0)
+
+    @pl.loop(1, n)
+    def _(i):
+        gate_copy(lax.rem(me + i, n)).start()
+
+    gate_buf[me] = gates[me]
+
     carry[...] = jnp.zeros_like(carry)
 
     @pl.loop(0, planes)
@@ -442,7 +443,7 @@
         def _():
             st_enter[quarter] = st_back[quarter]
 
-    for step in range(1, half - 1):
+    for step in range(1, half - 2):
         down.step(step)
 
     @pl.loop(1, 4)
@@ -506,18 +507,26 @@
             normed[2 * i] = both[:, :rows]
             normed[2 * i + 1] = both[:, rows:]
 
-    for step in range(half - 1, half):
+    for step in range(half - 2, half):
         down.step(step)
+    for step in range(-1, half - 1):
+        down.wait_side(step)
+    acc[...] = jnp.zeros_like(acc)
+
+    def project(place_of):
+        chip = ring_chip(chips, place_of)
+        for k in range(2):
+            slot = 2 * chip + k
+            acc[...] += jnp.dot(normed[slot], w_buf[slot], preferred_element_type=F32)
+
+    @pl.loop(0, chips - 1)
+    def _(i):
+        project(place + i + i // half)
+
     if skip:
         down.cross_step(half - 1)
-    for step in range(-1, half):
-        down.wait_side(step)
-    acc[...] = jnp.zeros_like(acc)
-
-    @pl.loop(0, n)
-    def _(i):
-        acc[...] += jnp.dot(normed[i], w_buf[i], preferred_element_type=F32)
-
+    down.wait_side(half - 1)
+    project(place + half)
     lat_buf[me] = acc[...].astype(BF16)
 
     lat = Gather(lat_buf, chips, place, core, (l_ring_s, l_ring_r, l_side_s, l_side_r))

time: 128 us -> 125 us (0.977)
  Pallas kernels: 121 us -> 118 us
    pallas_call x1, Pallas kernels: 121 us -> 118 us  [on_device(): pl.pallas_call(functools.partial(kernel, n, skip), out_shape=(jax.ShapeDt...]
where the time goes in v3:
time: 125 us
  Pallas kernels  118 us (94%)
  local copies, waits for them, and re-layouts  3.67 us (3%)
  other arithmetic  2.1 us (2%)
    pallas_call x1, Pallas kernels, on_device(): pl.pallas_call(functools.partial(kernel, n, skip), out_shape=(jax.ShapeDt...  118 us
    unnamed x4, local copies, waits for them, and re-layouts  3.04 us

profile of v3, /device:TPU:0, one launch (start us, length us, event | category | flops | bytes accessed | tf_op | source)
XLA Modules:
  0.0 124.5 jit_solution(7419624767688741917)
XLA Ops:
  0.6 0.7 convert_reduce_fusion
  1.3 0.7 convert_divide_fusion
  2.0 0.7 select_reduce_fusion
  2.7 0.6 broadcast_in_dim.24.gates
  3.4 118.1 %shard_map.131 = (bf16[128,4096]{1,0:T(8,128)(2,1)}, bf16[128,1024]{1,0:T(8,128)(2,1)}) custom-call(bf16[128,4096]{1,0:T(8,128)(2,1)} %values.1, bf16[128,512]{1,0:T(8,128)(2,1)} %in_b.1, bf16[128,512]{1,0:T(8,128)(2,1)} %out_c.1, f32[64,128]{1,0:T(8,128)} %decay_log.1, bf16[128,4096]{1,0:T(8,128)(2,1)} %residual.1, f32[1,4096]{1,0:T(1,128)} %bitcast.2, ...), custom_call_target="tpu_custom_call" | custom-call | tf_op jit(solution)/shard_map/pallas_call | solution.py:739
  121.5 0.0 copy-start
  121.5 2.3 %copy.18 = bf16[128,4096]{1,0:T(8,128)(2,1)} copy(bf16[128,4096]{1,0:T(8,128)(2,1)} %get-tuple-element.4) | data formatting | bytes 2097152
  123.8 0.0 copy-done
  123.8 0.7 copy.19
Async XLA Ops:
  121.5 2.3 %copy-start = (bf16[128,1024]{1,0:T(8,128)(2,1)S(1)}, bf16[128,1024]{1,0:T(8,128)(2,1)}, u32[]{:S(2)}) copy-start(bf16[128,1024]{1,0:T(8,128)(2,1)} %get-tuple-element.5) | copy-start | bytes 786436
